TPU v7x, 32 devices: a whole 2x2x4 slice. The times are simulated.
32 devices in a mesh: groups: 2 (over y), tp: 4 (over z), dp: 2 (over x), sub: 2 (over core).
Axes of the slice: x: 2, y: 2, z: 4, core: 2. Of those that a mesh axis runs over, the one named last changes fastest.
Arguments:
- queries: bfloat16 [32, 8192], P(('groups', 'dp', 'sub'), 'tp'), parts along dimension 0, may hold values from -8 to 8
- key_value_cache: bfloat16 [32, 2, 512, 1024], P(('groups', 'dp', 'sub'), None, 'tp'), parts along dimension 0, may hold values from -8 to 8
- fresh_token_entries: bfloat16 [32, 2, 1024], P(('groups', 'dp', 'sub')), parts along dimension 0, may hold values from -6 to 6
- lengths: int32 [32], P(('groups', 'dp', 'sub')), parts along dimension 0, may hold values from 128 to 512, as said below
- frozen_base_matrix: bfloat16 [8192, 5120], P('tp'), may hold values from -0.0625 to 0.0625
- lowrank_down_factor: bfloat16 [32, 8192], P('groups', ('tp', 'sub')), parts along dimension 0, may hold values from -0.375 to 0.375
- lowrank_up_factor: bfloat16 [32, 5120], P('groups', ('tp', 'sub')), parts along dimension 0, may hold values from -0.09375 to 0.09375
- magnitude: bfloat16 [10240], P(('groups', 'tp', 'sub')), parts along dimension 0, may hold values from 2 to 20
- piece_owner_blocks: int32 [16], P('groups'), parts along dimension 0, may hold values from 0 to 7, each once
Outputs:
- projected: bfloat16 [32, 5120], P(('groups', 'dp', 'sub'), 'tp'), parts along dimension 0
There are 2 independent parts, one for each index of `groups`. A program takes and returns all parts, laid end to end along the dimension named above; an argument that names none is the same for every part. Nothing has to cross between parts.
Inputs may be any that keep to these rules, and one draw needn't show every extreme that they name: piece_owner_blocks is a permutation. `lengths`: some sequence has all 512 positions cached.
All inputs are finite; a program needn't handle non-finite values.
Results may differ from a plain program's by a relative error of at most 0.0063.
Values may be sent and summed in bfloat16 or wider, within the bound.
A program may use at most 192 MiB of HBM per device.

v0:
```python
import jax
import jax.numpy as jnp
from jax import lax
from jax.sharding import PartitionSpec as P

HEADS = 64
KVH = 8
HD = 128
UPDATE_RANK = 16


norm_eps = 1e-06


def expand_rank(down_cols, up_rows):
    return lax.dot_general(
        down_cols, up_rows, (((0,), (0,)), ((), ())), preferred_element_type=jnp.float32
    )


def local(
    queries,
    key_value_cache,
    fresh_token_entries,
    lengths,
    frozen_base_matrix,
    lowrank_down_factor,
    lowrank_up_factor,
    magnitude,
    piece_owner_blocks,
):
    local_rows = frozen_base_matrix.shape[0]
    seq_count = queries.shape[0]
    cache_len = key_value_cache.shape[2]
    group_size = HEADS // KVH
    score_scale = HD ** (-0.5)
    tp_index = lax.axis_index("tp")
    down_all, up_all, magnitudes = (
        lax.all_gather(lowrank_down_factor, ("tp", "sub"), axis=1, tiled=True),
        lax.all_gather(lowrank_up_factor, ("tp", "sub"), axis=1, tiled=True),
        lax.all_gather(magnitude, ("tp", "sub"), axis=0, tiled=True),
    )
    piece_count = piece_owner_blocks.shape[0]
    rollout_block_rows = down_all.shape[1] // piece_count
    blocks_own = local_rows // rollout_block_rows
    wanted = tp_index * blocks_own + jnp.arange(blocks_own)
    selector = (piece_owner_blocks[None, :] == wanted[:, None]).astype(jnp.bfloat16)
    down_local = (
        jnp.einsum(
            "jk,rkc->rjc",
            selector,
            down_all.reshape(UPDATE_RANK, piece_count, rollout_block_rows),
            preferred_element_type=jnp.float32,
        )
        .astype(jnp.bfloat16)
        .reshape(UPDATE_RANK, local_rows)
    )
    query_all = lax.all_gather(queries, "tp", axis=1, tiled=True).reshape(
        seq_count, KVH, group_size, HD
    )
    keys_local = key_value_cache[:, 0].reshape(seq_count, cache_len, KVH, HD)
    values_local = key_value_cache[:, 1].reshape(seq_count, cache_len, KVH, HD)
    positions = tp_index * cache_len + jnp.arange(cache_len)
    valid_mask = positions[None, :] < lengths[:, None]
    scores = (
        jnp.einsum("skgd,spkd->skgp", query_all, keys_local, preferred_element_type=jnp.float32)
        * score_scale
    )
    scores = jnp.where(valid_mask[:, None, None, :], scores, -1e30)
    peak_part = lax.pmax(jnp.max(scores, axis=-1), "tp")
    new_key = fresh_token_entries[:, 0].reshape(seq_count, KVH, HD)
    new_value = fresh_token_entries[:, 1].reshape(seq_count, KVH, HD).astype(jnp.float32)
    own_score = (
        jnp.einsum("skgd,skd->skg", query_all, new_key, preferred_element_type=jnp.float32)
        * score_scale
    )
    peak_all = jnp.maximum(peak_part, own_score)
    weights = jnp.where(valid_mask[:, None, None, :], jnp.exp(scores - peak_all[..., None]), 0.0)
    weighted = jnp.einsum(
        "skgp,spkd->skgd",
        weights.astype(jnp.bfloat16),
        values_local,
        preferred_element_type=jnp.float32,
    )
    weights_sum = jnp.sum(weights, axis=-1)
    combined = frozen_base_matrix.astype(jnp.float32) + expand_rank(down_local, up_all)
    square_part = jnp.sum(combined * combined, axis=0)
    own_weight = jnp.exp(own_score - peak_all)
    own_rounded = lax.optimization_barrier(own_weight.astype(jnp.bfloat16)).astype(jnp.float32)
    column_total = lax.psum(square_part, "tp")
    weighted_all, weights_all = lax.psum((weighted, weights_sum), "tp")
    numer = weighted_all + own_rounded[..., None] * new_value[:, :, None, :]
    denom = weights_all + own_weight
    context = (numer / denom[..., None]).reshape(seq_count, HEADS * HD).astype(jnp.bfloat16)
    context_local = lax.dynamic_slice_in_dim(context, tp_index * local_rows, local_rows, 1)
    column_norms = jnp.sqrt(column_total + norm_eps)
    merged_matrix = (combined * (magnitudes.astype(jnp.float32) / column_norms)).astype(
        jnp.bfloat16
    )
    partial_out = jnp.dot(context_local, merged_matrix, preferred_element_type=jnp.float32)
    return lax.psum_scatter(partial_out, "tp", scatter_dimension=1, tiled=True).astype(jnp.bfloat16)


def solution(mesh):
    in_specs = (
        P(("groups", "dp", "sub"), "tp"),
        P(("groups", "dp", "sub"), None, "tp", None),
        P(("groups", "dp", "sub"), None, None),
        P(("groups", "dp", "sub")),
        P("tp", None),
        P("groups", ("tp", "sub")),
        P("groups", ("tp", "sub")),
        P(("groups", "tp", "sub")),
        P("groups"),
    )
    out_specs = P(("groups", "dp", "sub"), "tp")
    return jax.shard_map(local, mesh=mesh, in_specs=in_specs, out_specs=out_specs, check_vma=False)
```

profile of v0, /device:TPU:0, one launch (start us, length us, event | category | flops | bytes accessed | tf_op | source)
XLA Modules:
  0.0 214.1 jit_solution(5411967367081450215)
XLA Ops:
  6.5 0.0 all-reduce.3.cloned.1.call-start
  6.5 15.1 %all_gather.12 = bf16[4,8192]{1,0:T(4,128)(2,1)S(1)} all-gather(bf16[4,2048]{1,0:T(4,128)(2,1)} %param.9), channel_id=1, replica_groups=mesh['groups'=2,'tp'=4,'dp'=2,'sub'=2] {'tp'}, dimensions={1}, use_global_device_ids=true | all-gather | bytes 81920 | tf_op jit(solution)/shard_map/all_gather | solution.py:58
  21.6 1.8 fusion.28
  23.5 0.7 copy.25
  24.1 0.7 copy.24
  24.8 0.7 broadcast_compare_fusion
  25.5 0.9 fusion.8
  26.4 0.5 fusion.29
  26.9 18.9 %pmax.7 = f32[4,8,8]{2,1,0:T(8,128)S(1)} all-reduce(f32[4,8,8]{2,1,0:T(8,128)S(1)} %get-tuple-element.13), channel_id=1, replica_groups=mesh['groups'=2,'tp'=4,'dp'=2,'sub'=2] {'tp'}, use_global_device_ids=true, to_apply=%region_1.2 | all-reduce | flops 256 | bytes 2048 | tf_op jit(solution)/shard_map/pmax | solution.py:70
  45.7 1.3 fusion.6
  47.1 0.0 all-reduce.3.cloned.1.call-update
  47.1 0.0 reduce-scatter.4.cloned.1.call-start
  47.2 0.2 fusion.4
  47.4 0.7 reshape.58
  48.1 13.8 %all-gather = bf16[8,1,640]{2,1,0:T(2,128)(2,1)S(1)} all-gather(bf16[1,1,640]{2,1,0:T(2,128)(2,1)S(1)} %reshape.58), channel_id=1, replica_groups=mesh['groups'=2,'tp'=4,'dp'=2,'sub'=2] {'tp','sub'}, dimensions={0}, use_global_device_ids=true | all-gather | bytes 11520 | tf_op jit(solution)/shard_map/all_gather | solution.py:41
  61.9 14.4 %all_gather.14 = bf16[16,5120]{1,0:T(8,128)(2,1)S(1)} all-gather(bf16[16,640]{1,0:T(8,128)(2,1)} %param.15), channel_id=1, replica_groups=mesh['groups'=2,'tp'=4,'dp'=2,'sub'=2] {'tp','sub'}, dimensions={1}, use_global_device_ids=true | all-gather | bytes 184320 | tf_op jit(solution)/shard_map/all_gather | solution.py:40
  76.3 14.4 %all_gather.13 = bf16[16,8192]{1,0:T(8,128)(2,1)S(1)} all-gather(bf16[16,1024]{1,0:T(8,128)(2,1)} %param.14), channel_id=1, replica_groups=mesh['groups'=2,'tp'=4,'dp'=2,'sub'=2] {'tp','sub'}, dimensions={1}, use_global_device_ids=true | all-gather | bytes 294912 | tf_op jit(solution)/shard_map/all_gather | solution.py:39
  90.7 0.0 copy-start
  90.7 0.1 copy.28
  90.9 0.9 convolution_convert_fusion
  91.8 21.3 %multiply_reduce_fusion = (f32[5120]{0:T(1024)S(1)}, f32[2048,5120]{1,0:T(8,128)}) fusion(bf16[2048,5120]{1,0:T(8,128)(2,1)} %param.13, bf16[16,2048]{1,0:T(8,128)(2,1)S(1)} %bitcast.45, bf16[16,5120]{1,0:T(8,128)(2,1)S(1)} %all_gather.14), kind=kOutput, calls=%fused_computation.1 | convolution fusion | flops 377482240 | bytes 63164416 | tf_op jit(solution)/shard_map/dot_general | solution.py:16
  113.2 16.5 %all-reduce = (f32[5120]{0:T(1024)S(1)}, f32[4,8,8]{2,1,0:T(8,128)S(1)}) all-reduce(f32[5120]{0:T(1024)S(1)} %get-tuple-element.11, f32[4,8,8]{2,1,0:T(8,128)S(1)} %fusion.4), channel_id=1, replica_groups=mesh['groups'=2,'tp'=4,'dp'=2,'sub'=2] {'tp'}, use_global_device_ids=true, to_apply=%region_6.7 | all-reduce | flops 5376 | bytes 43008 | tf_op jit(solution)/shard_map/psum | solution.py:90
  129.8 0.0 copy-done
  129.8 0.0 all-reduce.3.cloned.1.call-done
  129.8 1.0 fusion.13
  130.9 0.1 copy.41
  130.9 23.1 %fusion.2 = f32[5120,4]{1,0:T(8,128)} fusion(f32[2048,5120]{1,0:T(8,128)} %get-tuple-element.12, bf16[2048,5120]{1,0:T(8,128)(2,1)} %param.13, f32[5120]{0:T(1024)S(1)} %rsqrt_multiply_fusion, bf16[4,8192]{1,0:T(4,128)(2,1)S(1)} %bitcast.49, s32[]{:T(128)S(6)} %select_n.12), kind=kOutput, calls=%fused_computation.5 | convolution fusion | flops 125829120 | bytes 63033348
  154.0 0.0 reduce-scatter.4.cloned.1.call-update
  154.0 51.4 %reduce-scatter.4.cloned.1.call-done = f32[1280,4]{1,0:T(8,128)} async-done(((f32[5120,4]{1,0:T(8,128)}), f32[1280,4]{1,0:T(8,128)}) %reduce-scatter.4.cloned.1.call-update) | async-done | bytes 20496
  205.4 1.9 copy.23
  (9 shorter events, 0.1 us)
Async XLA Ops:
  6.5 123.3 %all-reduce.3.cloned.1.call-start = ((), (), s32[]{:S(2)}) async-start(), calls=%async_computation.1 | async-start | bytes 262144 | tf_op jit(solution)/shard_map/psum | solution.py:91
  47.1 158.3 %reduce-scatter.4.cloned.1.call-start = ((), (), s32[]{:S(2)}) async-start(), calls=%async_computation.2 | async-start | bytes 3276800
  90.7 39.0 %copy-start = (bf16[4,2,1024]{2,1,0:T(2,128)(2,1)S(1)}, bf16[4,2,1024]{2,1,0:T(2,128)(2,1)}, u32[]{:S(2)}) copy-start(bf16[4,2,1024]{2,1,0:T(2,128)(2,1)} %param.11) | copy-start | bytes 49156
Sparse Core Ops, SparseCore 0:
  47.2 32.6 all-reduce.2
  154.1 51.1 reduce-scatter.3
where the time goes:
time: 215 us; the launch traced here: 214 us
  blocking collectives  93.1 us (43%)
  waiting for transfers between devices  51.4 us (24%)
  matrix products  48 us (22%)
  between operations  13.5 us (6%)
  local copies, waits for them, and re-layouts  5.97 us (3%)
    unnamed x3, waiting for transfers between devices  51.4 us
    unnamed x1, matrix products  23.1 us
    dot_general x1, matrix products, expand_rank(): lax.dot_general(down_cols, up_rows, (((0,), (0,)), ((), ())), preferred_e...  21.3 us
    pmax x1, blocking collectives, local(): peak_part = lax.pmax(jnp.max(scores, axis=-1), 'tp')  18.9 us
    psum x1, blocking collectives, local(): column_total = lax.psum(square_part, 'tp')  16.5 us
    all_gather x1, blocking collectives, local(): lax.all_gather(queries, 'tp', axis=1, tiled=True)  15.1 us
    all_gather x1, blocking collectives, local(): lax.all_gather(lowrank_down_factor, ('tp', 'sub'), axis=1, tiled=True)  14.4 us
    all_gather x1, blocking collectives, local(): lax.all_gather(lowrank_up_factor, ('tp', 'sub'), axis=1, tiled=True)  14.4 us
  transfers between devices with their start and end apart: 2, of which 1 were waited for; matrix products, arithmetic and copies ran while one was open for 11% of the time, Pallas kernels for 0%

commit v1 on v0

--- a/solution.py
+++ b/solution.py
@@ -1,6 +1,10 @@
+import functools
+
 import jax
 import jax.numpy as jnp
 from jax import lax
+from jax.experimental import pallas as pl
+from jax.experimental.pallas import tpu as pltpu
 from jax.sharding import PartitionSpec as P
 
 HEADS = 64
@@ -101,6 +105,522 @@
     return lax.psum_scatter(partial_out, "tp", scatter_dimension=1, tiled=True).astype(jnp.bfloat16)
 
 
+def fused_kernel(
+    sizes,
+    lengths_ref,
+    owner_ref,
+    query_ref,
+    fresh_ref,
+    down_ref,
+    up_ref,
+    magnitude_ref,
+    cache_ref,
+    base_ref,
+    out_ref,
+    query_f32,
+    query_all,
+    cache,
+    base,
+    combined,
+    pieces,
+    down_local,
+    up,
+    magnitudes,
+    part_send,
+    part_recv,
+    context_all,
+    context_f32,
+    norm_acc,
+    norm_send,
+    norm_recv,
+    proj_send,
+    proj_recv,
+    cache_sem,
+    base_sem,
+    query_s,
+    query_r,
+    piece_s,
+    piece_r,
+    forward_s,
+    forward_r,
+    up_s,
+    up_r,
+    mag_s,
+    mag_r,
+    part_s,
+    part_r,
+    context_s,
+    context_r,
+    norm_s,
+    norm_r,
+    proj_s,
+    proj_r,
+):
+    tp, dp, sub = sizes["tp"], sizes["dp"], sizes["sub"]
+    owners = dp * sub
+    t, d, s = lax.axis_index("tp"), lax.axis_index("dp"), lax.axis_index("sub")
+    q = d * sub + s
+    other = 1 - s
+    seqs = query_ref.shape[0]
+    heads = HEADS // tp
+    half = heads // 2
+    rows, columns = base.shape
+    cache_len = cache.shape[2]
+    score_scale = HD ** (-0.5)
+    f32, bf16 = jnp.float32, jnp.bfloat16
+
+    def place(tp_index, owner):
+        return {"tp": tp_index, "dp": owner // sub, "sub": lax.rem(owner, sub)}
+
+    def remote(src, dst, send, recv, where):
+        return pltpu.make_async_remote_copy(
+            src_ref=src,
+            dst_ref=dst,
+            send_sem=send,
+            recv_sem=recv,
+            device_id=where,
+            device_id_type=pl.DeviceIdType.MESH,
+        )
+
+    cache_copies = [
+        pltpu.make_async_copy(cache_ref.at[:, i], cache.at[:, i], cache_sem.at[i]) for i in range(2)
+    ]
+    for copy in cache_copies:
+        copy.start()
+    base_copy = pltpu.make_async_copy(
+        base_ref.at[:, pl.ds(pl.multiple_of(q * columns, columns), columns)], base, base_sem
+    )
+    base_copy.start()
+
+    barrier = pltpu.get_barrier_semaphore()
+    for r in range(tp):
+        for k in range(owners):
+            if r or k:
+                pl.semaphore_signal(
+                    barrier,
+                    inc=1,
+                    device_id=place(lax.rem(t + r, tp), lax.rem(q + k, owners)),
+                    device_id_type=pl.DeviceIdType.MESH,
+                )
+
+    for h in range(heads):
+        query_f32[pl.ds(h, seqs, stride=heads), :] = query_ref[:, h * HD : (h + 1) * HD].astype(f32)
+    own_query = query_f32[...].reshape(seqs, heads, HD)
+    query_all[t] = own_query.astype(bf16)
+    pieces[t * sub + s] = down_ref[...]
+    magnitudes[s] = magnitude_ref[...].astype(f32)
+
+    pl.semaphore_wait(barrier, tp * owners - 1)
+
+    query_copies, piece_copies = [], []
+    for r in range(1, tp):
+        peer = lax.rem(t + r, tp)
+        copy = remote(
+            query_all.at[t], query_all.at[t], query_s.at[r], query_r.at[t], place(peer, q)
+        )
+        copy.start()
+        query_copies.append(copy)
+    mag_copy = remote(
+        magnitudes.at[s], magnitudes.at[s], mag_s, mag_r, place(t, d * sub + other)
+    )
+    for r in range(1, tp):
+        peer = lax.rem(t + r, tp)
+        mine = t * sub + s
+        copy = remote(pieces.at[mine], pieces.at[mine], piece_s.at[r], piece_r.at[t], place(peer, q))
+        copy.start()
+        piece_copies.append(copy)
+
+    def forward(tp_index):
+        which = tp_index * sub + s
+        return remote(
+            pieces.at[which],
+            pieces.at[which],
+            forward_s.at[tp_index],
+            forward_r.at[tp_index],
+            place(t, d * sub + other),
+        )
+
+    forward(t).start()
+    mag_copy.start()
+
+    up_here = d == t // sub
+    up_owner = lax.rem(t, sub)
+
+    def up_copy(r):
+        return remote(
+            up_ref, up.at[s], up_s.at[r], up_r.at[s], place(lax.rem(t + r, tp), t)
+        )
+
+    up_self = jnp.logical_and(up_here, s == up_owner)
+
+    @pl.when(up_here)
+    def _():
+        for r in range(1, tp):
+            up_copy(r).start()
+
+    @pl.when(jnp.logical_and(up_here, s != up_owner))
+    def _():
+        up_copy(0).start()
+
+    @pl.when(up_self)
+    def _():
+        up[s] = up_ref[...]
+
+    row_index = lax.broadcasted_iota(jnp.int32, (heads, HD), 0)
+    lane_index = lax.broadcasted_iota(jnp.int32, (heads, HD), 1)
+    upper = row_index < half
+    position = t * cache_len + lax.broadcasted_iota(jnp.int32, (heads, cache_len), 1)
+
+    for copy in cache_copies:
+        copy.wait()
+
+    def attend(tp_index):
+        span = pl.ds(pl.multiple_of(tp_index * 2 * HD, 2 * HD), 2 * HD)
+        stats = jnp.zeros((heads, HD), f32)
+        for i in range(seqs):
+            query = query_all[tp_index, i].astype(f32)
+            left = jnp.where(upper, query, 0.0).astype(bf16)
+            right = jnp.where(upper, 0.0, query).astype(bf16)
+            scores = (
+                lax.dot_general(
+                    jnp.concatenate([left, right], axis=1),
+                    cache[i, 0, :, span],
+                    (((1,), (1,)), ((), ())),
+                    preferred_element_type=f32,
+                )
+                * score_scale
+            )
+            valid = position < lengths_ref[i]
+            scores = jnp.where(valid, scores, -1e30)
+            peak = jnp.max(scores, axis=-1, keepdims=True)
+            weights = jnp.where(valid, jnp.exp(scores - peak), 0.0)
+            total = jnp.sum(weights, axis=-1, keepdims=True)
+            both = jnp.dot(
+                weights.astype(bf16), cache[i, 1, :, span], preferred_element_type=f32
+            )
+            part_send[tp_index, i] = jnp.where(upper, both[:, :HD], both[:, HD:])
+            stats = jnp.where(lane_index == i, peak, stats)
+            stats = jnp.where(lane_index == seqs + i, total, stats)
+        part_send[tp_index, seqs] = stats
+
+    attend(t)
+    part_recv[t] = part_send[t]
+    part_copies = []
+    for r in range(1, tp):
+        peer = lax.rem(t + tp - r, tp)
+        remote(
+            query_all.at[peer], query_all.at[peer], query_s.at[r], query_r.at[peer], place(peer, q)
+        ).wait_recv()
+        attend(peer)
+        copy = remote(
+            part_send.at[peer], part_recv.at[t], part_s.at[r], part_r.at[t], place(peer, q)
+        )
+        copy.start()
+        part_copies.append(copy)
+
+    for r in range(1, tp):
+        peer = lax.rem(t + tp - r, tp)
+        which = peer * sub + s
+        remote(
+            pieces.at[which], pieces.at[which], piece_s.at[r], piece_r.at[peer], place(peer, q)
+        ).wait_recv()
+        forward(peer).start()
+
+    for j in range(sub):
+
+        @pl.when(jnp.logical_or(t != q, s != j))
+        def _():
+            remote(up_ref, up.at[j], up_s.at[0], up_r.at[j], place(t, q)).wait_recv()
+
+    for r in range(tp):
+        peer = lax.rem(t + r, tp)
+        which = peer * sub + other
+        remote(
+            pieces.at[which],
+            pieces.at[which],
+            forward_s.at[peer],
+            forward_r.at[peer],
+            place(t, d * sub + other),
+        ).wait_recv()
+
+    piece_rows = pieces.shape[2]
+    for j in range(rows // piece_rows):
+        wanted = t * (rows // piece_rows) + j
+        found = jnp.int32(0)
+        for k in range(pieces.shape[0]):
+            found = jnp.where(owner_ref[k] == wanted, k, found)
+        down_local[:, j * piece_rows : (j + 1) * piece_rows] = pieces[found]
+
+    base_copy.wait()
+    norm_acc[...] = jnp.zeros_like(norm_acc)
+    block = 256
+    up_all = jnp.concatenate([up[j] for j in range(sub)], axis=1)
+
+    def merge(c, carry):
+        here = pl.ds(pl.multiple_of(c * block, block), block)
+        down_rows = down_local[:, here]
+        for n in range(columns // block):
+            cols = slice(n * block, (n + 1) * block)
+            tile = base[here, cols].astype(f32) + lax.dot_general(
+                down_rows, up_all[:, cols], (((0,), (0,)), ((), ())), preferred_element_type=f32
+            )
+            norm_acc[:, cols] += jnp.sum((tile * tile).reshape(block // 8, 8, block), axis=0)
+            combined[here, cols] = tile.astype(bf16)
+        return carry
+
+    lax.fori_loop(0, rows // block, merge, 0)
+    norm_send[...] = jnp.sum(norm_acc[...], axis=0, keepdims=True)
+
+    def result_copy(src, dst, send, recv, k):
+        return remote(
+            src, dst.at[t], send.at[k], recv.at[t], place(q, lax.rem(q + k, owners))
+        )
+
+    itself = t == q
+
+    def norm_copy(k):
+        return result_copy(norm_send, norm_recv, norm_s, norm_r, k)
+
+    for k in range(1, owners):
+        norm_copy(k).start()
+
+    @pl.when(jnp.logical_not(itself))
+    def _():
+        norm_copy(0).start()
+
+    @pl.when(itself)
+    def _():
+        norm_recv[t] = norm_send[...]
+
+    fresh = [
+        [
+            fresh_ref[
+                i, :, pl.ds(pl.multiple_of((t * 2 + j) * HD, HD), HD)
+            ].astype(f32)
+            for j in range(2)
+        ]
+        for i in range(seqs)
+    ]
+    own_scores, own_values = [], []
+    for i in range(seqs):
+        key = jnp.where(upper, fresh[i][0][0:1], fresh[i][1][0:1])
+        own_values.append(jnp.where(upper, fresh[i][0][1:2], fresh[i][1][1:2]))
+        rows_of_query = query_f32[i * heads : (i + 1) * heads, :]
+        own_scores.append(jnp.sum(rows_of_query * key, axis=-1, keepdims=True) * score_scale)
+
+    for r in range(1, tp):
+        peer = lax.rem(t + r, tp)
+        remote(
+            part_send.at[peer], part_recv.at[peer], part_s.at[r], part_r.at[peer], place(peer, q)
+        ).wait_recv()
+
+    all_stats = [part_recv[k, seqs] for k in range(tp)]
+    for i in range(seqs):
+        peaks = [x[:, i : i + 1] for x in all_stats]
+        peak = own_scores[i]
+        for x in peaks:
+            peak = jnp.maximum(peak, x)
+        own_weight = jnp.exp(own_scores[i] - peak)
+        numer = own_weight.astype(bf16).astype(f32) * own_values[i]
+        denom = own_weight
+        for k in range(tp):
+            factor = jnp.exp(peaks[k] - peak)
+            numer = numer + factor * part_recv[k, i]
+            denom = denom + factor * all_stats[k][:, seqs + i : seqs + i + 1]
+        context_all[q, i] = (numer / denom).astype(bf16)
+
+    context_copies = []
+    for k in range(1, owners):
+        copy = remote(
+            context_all.at[q],
+            context_all.at[q],
+            context_s.at[k],
+            context_r.at[q],
+            place(t, lax.rem(q + k, owners)),
+        )
+        copy.start()
+        context_copies.append(copy)
+    for k in range(1, owners):
+        peer = lax.rem(q + k, owners)
+        remote(
+            context_all.at[peer],
+            context_all.at[peer],
+            context_s.at[k],
+            context_r.at[peer],
+            place(t, peer),
+        ).wait_recv()
+
+    total_seqs = owners * seqs
+    context_f32[...] = context_all[...].astype(f32).reshape(total_seqs * heads, HD)
+    context = jnp.concatenate(
+        [context_f32[pl.ds(h, total_seqs, stride=heads), :].astype(bf16) for h in range(heads)],
+        axis=1,
+    )
+    middle = columns // 2
+    for n in range(columns // block):
+        partial = jnp.dot(
+            context, combined[:, n * block : (n + 1) * block], preferred_element_type=f32
+        )
+        for piece in range(block // HD):
+            start = n * block + piece * HD
+            side, lane = start // middle, start % middle
+            for k in range(owners):
+                proj_send[k, side * seqs : (side + 1) * seqs, lane : lane + HD] = partial[
+                    k * seqs : (k + 1) * seqs, piece * HD : (piece + 1) * HD
+                ]
+
+    def proj_copy(k):
+        return result_copy(
+            proj_send.at[lax.rem(q + k, owners)], proj_recv, proj_s, proj_r, k
+        )
+
+    for k in range(1, owners):
+        proj_copy(k).start()
+
+    @pl.when(jnp.logical_not(itself))
+    def _():
+        proj_copy(0).start()
+
+    @pl.when(itself)
+    def _():
+        proj_recv[t] = proj_send[q]
+
+    remote(
+        magnitudes.at[other], magnitudes.at[other], mag_s, mag_r, place(t, d * sub + other)
+    ).wait_recv()
+
+    def arrived(src, dst, send, recv):
+        for k in range(tp):
+
+            @pl.when(jnp.logical_or(q != t, t != k))
+            def _():
+                remote(src, dst.at[k], send.at[0], recv.at[k], place(k, t)).wait_recv()
+
+    arrived(norm_send, norm_recv, norm_s, norm_r)
+    squares = norm_recv[0]
+    for k in range(1, tp):
+        squares = squares + norm_recv[k]
+    norms = jnp.sqrt(squares + norm_eps)
+    arrived(proj_send.at[0], proj_recv, proj_s, proj_r)
+    total = proj_recv[0]
+    for k in range(1, tp):
+        total = total + proj_recv[k]
+    for side in range(2):
+        scale = magnitudes[side] / norms[:, side * middle : (side + 1) * middle]
+        out_ref[:, side * middle : (side + 1) * middle] = (
+            total[side * seqs : (side + 1) * seqs] * scale
+        ).astype(bf16)
+
+    for copy in query_copies + piece_copies + part_copies + context_copies:
+        copy.wait_send()
+    mag_copy.wait_send()
+    for r in range(tp):
+        forward(lax.rem(t + r, tp)).wait_send()
+
+    @pl.when(up_here)
+    def _():
+        for r in range(1, tp):
+            up_copy(r).wait_send()
+
+    @pl.when(jnp.logical_and(up_here, s != up_owner))
+    def _():
+        up_copy(0).wait_send()
+
+    for k in range(1, owners):
+        norm_copy(k).wait_send()
+        proj_copy(k).wait_send()
+
+    @pl.when(jnp.logical_not(itself))
+    def _():
+        norm_copy(0).wait_send()
+        proj_copy(0).wait_send()
+
+
+def fused_local(
+    sizes,
+    queries,
+    key_value_cache,
+    fresh_token_entries,
+    lengths,
+    frozen_base_matrix,
+    lowrank_down_factor,
+    lowrank_up_factor,
+    magnitude,
+    piece_owner_blocks,
+):
+    tp, dp, sub = sizes["tp"], sizes["dp"], sizes["sub"]
+    owners = dp * sub
+    seqs = queries.shape[0]
+    heads = HEADS // tp
+    rows, width = frozen_base_matrix.shape
+    columns = width // owners
+    trainers = tp * sub
+    f32, bf16 = jnp.float32, jnp.bfloat16
+    sem = pltpu.SemaphoreType.DMA
+    vmem = pl.BlockSpec(memory_space=pltpu.VMEM)
+    smem = pl.BlockSpec(memory_space=pltpu.SMEM)
+    anywhere = pl.BlockSpec(memory_space=pl.ANY)
+    return pl.pallas_call(
+        functools.partial(fused_kernel, sizes),
+        out_shape=jax.ShapeDtypeStruct((seqs, width // tp), bf16),
+        in_specs=[smem, smem, vmem, vmem, vmem, vmem, vmem, anywhere, anywhere],
+        out_specs=vmem,
+        scratch_shapes=[
+            pltpu.VMEM((seqs * heads, HD), f32),
+            pltpu.VMEM((tp, seqs, heads, HD), bf16),
+            pltpu.VMEM(key_value_cache.shape, bf16),
+            pltpu.VMEM((rows, columns), bf16),
+            pltpu.VMEM((rows, columns), bf16),
+            pltpu.VMEM((trainers,) + lowrank_down_factor.shape, bf16),
+            pltpu.VMEM((UPDATE_RANK, rows), bf16),
+            pltpu.VMEM((sub,) + lowrank_up_factor.shape, bf16),
+            pltpu.VMEM((sub, 1, magnitude.shape[0]), f32),
+            pltpu.VMEM((tp, seqs + 1, heads, HD), f32),
+            pltpu.VMEM((tp, seqs + 1, heads, HD), f32),
+            pltpu.VMEM((owners, seqs, heads, HD), bf16),
+            pltpu.VMEM((owners * seqs * heads, HD), f32),
+            pltpu.VMEM((8, columns), f32),
+            pltpu.VMEM((1, columns), f32),
+            pltpu.VMEM((tp, 1, columns), f32),
+            pltpu.VMEM((owners, 2 * seqs, columns // 2), f32),
+            pltpu.VMEM((tp, 2 * seqs, columns // 2), f32),
+            sem((2,)),
+            sem,
+            sem((tp,)),
+            sem((tp,)),
+            sem((tp,)),
+            sem((tp,)),
+            sem((tp,)),
+            sem((tp,)),
+            sem((tp,)),
+            sem((sub,)),
+            sem,
+            sem,
+            sem((tp,)),
+            sem((tp,)),
+            sem((owners,)),
+            sem((owners,)),
+            sem((owners,)),
+            sem((tp,)),
+            sem((owners,)),
+            sem((tp,)),
+        ],
+        compiler_params=pltpu.CompilerParams(
+            collective_id=0, has_side_effects=True, vmem_limit_bytes=56 * 1024 * 1024
+        ),
+    )(
+        lengths,
+        piece_owner_blocks,
+        queries,
+        fresh_token_entries,
+        lowrank_down_factor,
+        lowrank_up_factor,
+        magnitude.reshape(1, -1),
+        key_value_cache,
+        frozen_base_matrix,
+    )
+
+
 def solution(mesh):
     in_specs = (
         P(("groups", "dp", "sub"), "tp"),
@@ -114,4 +634,8 @@
         P("groups"),
     )
     out_specs = P(("groups", "dp", "sub"), "tp")
-    return jax.shard_map(local, mesh=mesh, in_specs=in_specs, out_specs=out_specs, check_vma=False)
+    sizes = dict(mesh.shape)
+    owners = sizes["dp"] * sizes["sub"]
+    fits = sizes["tp"] == owners and 2 * sizes["tp"] == KVH and sizes["sub"] == 2
+    body = functools.partial(fused_local, sizes) if fits else local
+    return jax.shard_map(body, mesh=mesh, in_specs=in_specs, out_specs=out_specs, check_vma=False)

time: 215 us -> 30.6 us (0.14)
  blocking collectives: 93.1 us -> 0 us
  waiting for transfers between devices: 51.4 us -> 0 us
  matrix products: 48 us -> 0 us
  Pallas kernels: 0 us -> 27.8 us
  between operations: 13.5 us -> 0.01 us
  local copies, waits for them, and re-layouts: 5.97 us -> 2.57 us
    all_gather x4 -> x0, blocking collectives: 57.7 us -> none  [the longest x1 15.1 us: local(): lax.all_gather(queries, 'tp', axis=1, tiled=True)]
    unnamed x3 -> x0, waiting for transfers between devices: 51.4 us -> none
    pallas_call x0 -> x1, Pallas kernels: none -> 27.8 us  [fused_local(): pl.pallas_call(functools.partial(fused_kernel, sizes), out_shape=jax.Shap...]
    dot_general x5 -> x0, matrix products: 24.9 us -> none  [the longest x1 21.3 us: expand_rank(): lax.dot_general(down_cols, up_rows, (((0,), (0,)), ((), ())), preferred_e...]
    unnamed x1 -> x0, matrix products: 23.1 us -> none
    pmax x1 -> x0, blocking collectives: 18.9 us -> none  [local(): peak_part = lax.pmax(jnp.max(scores, axis=-1), 'tp')]
    psum x1 -> x0, blocking collectives: 16.5 us -> none  [local(): column_total = lax.psum(square_part, 'tp')]
    unnamed x9 -> x1, local copies, waits for them, and re-layouts: 4.15 us -> 1.31 us
  transfers between devices with their start and end apart: 2 -> 0, of which waited for: 1 -> 0; matrix products, arithmetic and copies ran while one was open for 11% -> 0% of each run, Pallas kernels for 0% -> 0%
where the time goes in v1:
time: 30.6 us; the launch traced here: 30.4 us
  Pallas kernels  27.8 us (91%)
  local copies, waits for them, and re-layouts  2.57 us (8%)
    pallas_call x1, Pallas kernels, fused_local(): pl.pallas_call(functools.partial(fused_kernel, sizes), out_shape=jax.Shap...  27.8 us
    unnamed x1, local copies, waits for them, and re-layouts  1.31 us
    reshape x1, local copies, waits for them, and re-layouts, fused_local(): magnitude.reshape(1, -1)  1.26 us

profile of v1, /device:TPU:0, one launch (start us, length us, event | category | flops | bytes accessed | tf_op | source)
XLA Modules:
  0.0 30.4 jit_solution(5155161360086357895)
XLA Ops:
  0.0 1.3 %reshape.3.magnitude_ref = bf16[1,640]{1,0:T(2,128)(2,1)} reshape(bf16[640]{0:T(1024)(128)(2,1)} %param.16) | data formatting | bytes 2560 | tf_op jit(solution)/shard_map/reshape | solution.py:618
  1.3 27.8 %shard_map.91 = bf16[4,1280]{1,0:T(4,128)(2,1)} custom-call(s32[4]{0:T(128)} %lengths_ref.1, s32[8]{0:T(128)} %owner_ref.1, bf16[4,2048]{1,0:T(4,128)(2,1)} %query_ref.1, bf16[4,2,1024]{2,1,0:T(2,128)(2,1)} %fresh_ref.1, bf16[16,1024]{1,0:T(8,128)(2,1)} %down_ref.1, bf16[16,640]{1,0:T(8,128)(2,1)} %up_ref.1, bf16[1,640]{1,0:T(2,128)(2,1)} %reshape.3.magnitude_ref, ...), custom_call_target="tpu_custom_call" | custom-call | tf_op jit(solution)/shard_map/pallas_call | solution.py:563
  29.1 1.3 %copy.11 = bf16[4,1280]{1,0:T(4,128)(2,1)} copy(bf16[4,1280]{1,0:T(4,128)(2,1)} %shard_map.91) | data formatting | bytes 20480

commit v2 on v1

--- a/solution.py
+++ b/solution.py
@@ -145,6 +145,8 @@
     forward_r,
     up_s,
     up_r,
+    own_s,
+    own_r,
     mag_s,
     mag_r,
     part_s,
@@ -159,7 +161,7 @@
     tp, dp, sub = sizes["tp"], sizes["dp"], sizes["sub"]
     owners = dp * sub
     t, d, s = lax.axis_index("tp"), lax.axis_index("dp"), lax.axis_index("sub")
-    q = d * sub + s
+    q = d + dp * s
     other = 1 - s
     seqs = query_ref.shape[0]
     heads = HEADS // tp
@@ -170,7 +172,14 @@
     f32, bf16 = jnp.float32, jnp.bfloat16
 
     def place(tp_index, owner):
-        return {"tp": tp_index, "dp": owner // sub, "sub": lax.rem(owner, sub)}
+        return {"tp": tp_index, "dp": lax.rem(owner, dp), "sub": owner // dp}
+
+    def peer_of(r):
+        if r == 1:
+            return t + 1 - 2 * lax.rem(t, 2)
+        if r == 2:
+            return t + 2 - 4 * (t // 2)
+        return tp - 1 - t
 
     def remote(src, dst, send, recv, where):
         return pltpu.make_async_remote_copy(
@@ -193,78 +202,19 @@
     base_copy.start()
 
     barrier = pltpu.get_barrier_semaphore()
-    for r in range(tp):
-        for k in range(owners):
-            if r or k:
-                pl.semaphore_signal(
-                    barrier,
-                    inc=1,
-                    device_id=place(lax.rem(t + r, tp), lax.rem(q + k, owners)),
-                    device_id_type=pl.DeviceIdType.MESH,
-                )
+    greeted = [place(peer_of(r), q) for r in range(1, tp)]
+    greeted += [place(t, lax.rem(q + k, owners)) for k in range(1, owners)]
+    for where in greeted:
+        pl.semaphore_signal(
+            barrier, inc=1, device_id=where, device_id_type=pl.DeviceIdType.MESH
+        )
 
     for h in range(heads):
         query_f32[pl.ds(h, seqs, stride=heads), :] = query_ref[:, h * HD : (h + 1) * HD].astype(f32)
     own_query = query_f32[...].reshape(seqs, heads, HD)
     query_all[t] = own_query.astype(bf16)
     pieces[t * sub + s] = down_ref[...]
-    magnitudes[s] = magnitude_ref[...].astype(f32)
-
-    pl.semaphore_wait(barrier, tp * owners - 1)
-
-    query_copies, piece_copies = [], []
-    for r in range(1, tp):
-        peer = lax.rem(t + r, tp)
-        copy = remote(
-            query_all.at[t], query_all.at[t], query_s.at[r], query_r.at[t], place(peer, q)
-        )
-        copy.start()
-        query_copies.append(copy)
-    mag_copy = remote(
-        magnitudes.at[s], magnitudes.at[s], mag_s, mag_r, place(t, d * sub + other)
-    )
-    for r in range(1, tp):
-        peer = lax.rem(t + r, tp)
-        mine = t * sub + s
-        copy = remote(pieces.at[mine], pieces.at[mine], piece_s.at[r], piece_r.at[t], place(peer, q))
-        copy.start()
-        piece_copies.append(copy)
-
-    def forward(tp_index):
-        which = tp_index * sub + s
-        return remote(
-            pieces.at[which],
-            pieces.at[which],
-            forward_s.at[tp_index],
-            forward_r.at[tp_index],
-            place(t, d * sub + other),
-        )
-
-    forward(t).start()
-    mag_copy.start()
-
-    up_here = d == t // sub
-    up_owner = lax.rem(t, sub)
-
-    def up_copy(r):
-        return remote(
-            up_ref, up.at[s], up_s.at[r], up_r.at[s], place(lax.rem(t + r, tp), t)
-        )
-
-    up_self = jnp.logical_and(up_here, s == up_owner)
-
-    @pl.when(up_here)
-    def _():
-        for r in range(1, tp):
-            up_copy(r).start()
-
-    @pl.when(jnp.logical_and(up_here, s != up_owner))
-    def _():
-        up_copy(0).start()
-
-    @pl.when(up_self)
-    def _():
-        up[s] = up_ref[...]
+    magnitudes[s] = magnitude_ref[...].astype(f32).reshape(1, -1)
 
     row_index = lax.broadcasted_iota(jnp.int32, (heads, HD), 0)
     lane_index = lax.broadcasted_iota(jnp.int32, (heads, HD), 1)
@@ -273,6 +223,18 @@
 
     for copy in cache_copies:
         copy.wait()
+
+    def split3(value):
+        terms = []
+        for _ in range(3):
+            term = value.astype(bf16).astype(f32)
+            terms.append(term)
+            value = value - term
+        return terms
+
+    def joined(stats, first, i):
+        lanes = [stats[:, (first + n) * seqs + i : (first + n) * seqs + i + 1] for n in range(3)]
+        return (lanes[0] + lanes[1]) + lanes[2]
 
     def attend(tp_index):
         span = pl.ds(pl.multiple_of(tp_index * 2 * HD, 2 * HD), 2 * HD)
@@ -298,33 +260,98 @@
             both = jnp.dot(
                 weights.astype(bf16), cache[i, 1, :, span], preferred_element_type=f32
             )
-            part_send[tp_index, i] = jnp.where(upper, both[:, :HD], both[:, HD:])
-            stats = jnp.where(lane_index == i, peak, stats)
-            stats = jnp.where(lane_index == seqs + i, total, stats)
-        part_send[tp_index, seqs] = stats
+            part_send[tp_index, i] = jnp.where(upper, both[:, :HD], both[:, HD:]).astype(bf16)
+            for term, value in enumerate(split3(peak) + split3(total)):
+                stats = jnp.where(lane_index == term * seqs + i, value, stats)
+        part_send[tp_index, seqs] = stats.astype(bf16)
 
     attend(t)
     part_recv[t] = part_send[t]
+
+    pl.semaphore_wait(barrier, len(greeted))
+
+    sibling = place(t, d + dp * other)
+    mine = t * sub + s
+    piece_columns = pieces.shape[2] // dp
+
+    def part_of(piece, which_half):
+        return pieces.at[
+            piece, :, pl.ds(pl.multiple_of(which_half * piece_columns, piece_columns), piece_columns)
+        ]
+
+    query_copies, piece_copies = [], []
+    for r in (3, 2, 1):
+        copy = remote(
+            query_all.at[t], query_all.at[t], query_s.at[r], query_r.at[t], place(peer_of(r), q)
+        )
+        copy.start()
+        query_copies.append(copy)
+    for r in (3, 2, 1):
+        copy = remote(
+            part_of(mine, d),
+            part_of(mine, d),
+            piece_s.at[r],
+            piece_r.at[t],
+            place(peer_of(r), q),
+        )
+        copy.start()
+        piece_copies.append(copy)
+    for src, send, recv in ((pieces.at[mine], own_s, own_r), (magnitudes.at[s], mag_s, mag_r)):
+        copy = remote(src, src, send, recv, sibling)
+        copy.start()
+        piece_copies.append(copy)
+
+    up_here = d == lax.rem(t, dp)
+    up_owner = t // dp
+
+    def up_copy(r):
+        return remote(
+            up_ref, up.at[s], up_s.at[r], up_r.at[s], place(peer_of(r) if r else t, t)
+        )
+
+    up_self = jnp.logical_and(up_here, s == up_owner)
+
+    @pl.when(jnp.logical_and(up_here, s != up_owner))
+    def _():
+        up_copy(0).start()
+
+    @pl.when(up_self)
+    def _():
+        up[s] = up_ref[...]
+
     part_copies = []
     for r in range(1, tp):
-        peer = lax.rem(t + tp - r, tp)
+        peer = peer_of(r)
         remote(
             query_all.at[peer], query_all.at[peer], query_s.at[r], query_r.at[peer], place(peer, q)
         ).wait_recv()
         attend(peer)
+
+        @pl.when(up_here)
+        def _():
+            up_copy(r).start()
+
         copy = remote(
             part_send.at[peer], part_recv.at[t], part_s.at[r], part_r.at[t], place(peer, q)
         )
         copy.start()
         part_copies.append(copy)
 
+    forward_copies = []
     for r in range(1, tp):
-        peer = lax.rem(t + tp - r, tp)
-        which = peer * sub + s
-        remote(
-            pieces.at[which], pieces.at[which], piece_s.at[r], piece_r.at[peer], place(peer, q)
-        ).wait_recv()
-        forward(peer).start()
+        peer = peer_of(r)
+        got = part_of(peer * sub + s, d)
+        remote(got, got, piece_s.at[r], piece_r.at[peer], place(peer, q)).wait_recv()
+        for k in range(1, owners):
+            copy = remote(
+                got,
+                got,
+                forward_s.at[r, k],
+                forward_r.at[peer, q],
+                place(t, lax.rem(q + k, owners)),
+            )
+            copy.start()
+            forward_copies.append(copy)
 
     for j in range(sub):
 
@@ -332,16 +359,16 @@
         def _():
             remote(up_ref, up.at[j], up_s.at[0], up_r.at[j], place(t, q)).wait_recv()
 
-    for r in range(tp):
-        peer = lax.rem(t + r, tp)
-        which = peer * sub + other
-        remote(
-            pieces.at[which],
-            pieces.at[which],
-            forward_s.at[peer],
-            forward_r.at[peer],
-            place(t, d * sub + other),
-        ).wait_recv()
+    got = pieces.at[t * sub + other]
+    remote(got, got, own_s, own_r, sibling).wait_recv()
+    for r in range(1, tp):
+        peer = peer_of(r)
+        for k in range(1, owners):
+            source = lax.rem(q + k, owners)
+            got = part_of(peer * sub + source // dp, lax.rem(source, dp))
+            remote(
+                got, got, forward_s.at[r, k], forward_r.at[peer, source], place(t, source)
+            ).wait_recv()
 
     piece_rows = pieces.shape[2]
     for j in range(rows // piece_rows):
@@ -409,14 +436,14 @@
         own_scores.append(jnp.sum(rows_of_query * key, axis=-1, keepdims=True) * score_scale)
 
     for r in range(1, tp):
-        peer = lax.rem(t + r, tp)
+        peer = peer_of(r)
         remote(
             part_send.at[peer], part_recv.at[peer], part_s.at[r], part_r.at[peer], place(peer, q)
         ).wait_recv()
 
-    all_stats = [part_recv[k, seqs] for k in range(tp)]
+    all_stats = [part_recv[k, seqs].astype(f32) for k in range(tp)]
     for i in range(seqs):
-        peaks = [x[:, i : i + 1] for x in all_stats]
+        peaks = [joined(x, 0, i) for x in all_stats]
         peak = own_scores[i]
         for x in peaks:
             peak = jnp.maximum(peak, x)
@@ -425,8 +452,8 @@
         denom = own_weight
         for k in range(tp):
             factor = jnp.exp(peaks[k] - peak)
-            numer = numer + factor * part_recv[k, i]
-            denom = denom + factor * all_stats[k][:, seqs + i : seqs + i + 1]
+            numer = numer + factor * part_recv[k, i].astype(f32)
+            denom = denom + factor * joined(all_stats[k], 3, i)
         context_all[q, i] = (numer / denom).astype(bf16)
 
     context_copies = []
@@ -486,7 +513,7 @@
         proj_recv[t] = proj_send[q]
 
     remote(
-        magnitudes.at[other], magnitudes.at[other], mag_s, mag_r, place(t, d * sub + other)
+        magnitudes.at[other], magnitudes.at[other], mag_s, mag_r, sibling
     ).wait_recv()
 
     def arrived(src, dst, send, recv):
@@ -511,11 +538,8 @@
             total[side * seqs : (side + 1) * seqs] * scale
         ).astype(bf16)
 
-    for copy in query_copies + piece_copies + part_copies + context_copies:
+    for copy in query_copies + piece_copies + forward_copies + part_copies + context_copies:
         copy.wait_send()
-    mag_copy.wait_send()
-    for r in range(tp):
-        forward(lax.rem(t + r, tp)).wait_send()
 
     @pl.when(up_here)
     def _():
@@ -575,8 +599,8 @@
             pltpu.VMEM((UPDATE_RANK, rows), bf16),
             pltpu.VMEM((sub,) + lowrank_up_factor.shape, bf16),
             pltpu.VMEM((sub, 1, magnitude.shape[0]), f32),
-            pltpu.VMEM((tp, seqs + 1, heads, HD), f32),
-            pltpu.VMEM((tp, seqs + 1, heads, HD), f32),
+            pltpu.VMEM((tp, seqs + 1, heads, HD), bf16),
+            pltpu.VMEM((tp, seqs + 1, heads, HD), bf16),
             pltpu.VMEM((owners, seqs, heads, HD), bf16),
             pltpu.VMEM((owners * seqs * heads, HD), f32),
             pltpu.VMEM((8, columns), f32),
@@ -590,10 +614,12 @@
             sem((tp,)),
             sem((tp,)),
             sem((tp,)),
-            sem((tp,)),
-            sem((tp,)),
+            sem((tp, owners)),
+            sem((tp, owners)),
             sem((tp,)),
             sem((sub,)),
+            sem,
+            sem,
             sem,
             sem,
             sem((tp,)),
@@ -615,7 +641,7 @@
         fresh_token_entries,
         lowrank_down_factor,
         lowrank_up_factor,
-        magnitude.reshape(1, -1),
+        magnitude,
         key_value_cache,
         frozen_base_matrix,
     )

time: 30.6 us -> 31.2 us (1.020)
  Pallas kernels: 27.8 us -> 29.6 us
  local copies, waits for them, and re-layouts: 2.57 us -> 1.31 us
    pallas_call x1, Pallas kernels: 27.8 us -> 29.6 us  [fused_local(): pl.pallas_call(functools.partial(fused_kernel, sizes), out_shape=jax.Shap...]
    reshape x1 -> x0, local copies, waits for them, and re-layouts: 1.26 us -> none  [fused_local(): magnitude.reshape(1, -1)]
where the time goes in v2:
time: 31.2 us; the launch traced here: 30.9 us
  Pallas kernels  29.6 us (95%)
  local copies, waits for them, and re-layouts  1.31 us (4%)
    pallas_call x1, Pallas kernels, fused_local(): pl.pallas_call(functools.partial(fused_kernel, sizes), out_shape=jax.Shap...  29.6 us
    unnamed x1, local copies, waits for them, and re-layouts  1.31 us

profile of v2, /device:TPU:0, one launch (start us, length us, event | category | flops | bytes accessed | tf_op | source)
XLA Modules:
  0.0 30.9 jit_solution(3733480017886411996)
XLA Ops:
  0.0 29.6 %shard_map.91 = bf16[4,1280]{1,0:T(4,128)(2,1)} custom-call(s32[4]{0:T(128)} %lengths_ref.1, s32[8]{0:T(128)} %owner_ref.1, bf16[4,2048]{1,0:T(4,128)(2,1)} %query_ref.1, bf16[4,2,1024]{2,1,0:T(2,128)(2,1)} %fresh_ref.1, bf16[16,1024]{1,0:T(8,128)(2,1)} %down_ref.1, bf16[16,640]{1,0:T(8,128)(2,1)} %up_ref.1, bf16[640]{0:T(1024)(128)(2,1)} %magnitude_ref.1, ...), custom_call_target="tpu_custom_call" | custom-call | tf_op jit(solution)/shard_map/pallas_call | solution.py:587
  29.6 1.3 %copy.11 = bf16[4,1280]{1,0:T(4,128)(2,1)} copy(bf16[4,1280]{1,0:T(4,128)(2,1)} %shard_map.91) | data formatting | bytes 20480

commit v3 on v2

--- a/solution.py
+++ b/solution.py
@@ -353,72 +353,6 @@
             copy.start()
             forward_copies.append(copy)
 
-    for j in range(sub):
-
-        @pl.when(jnp.logical_or(t != q, s != j))
-        def _():
-            remote(up_ref, up.at[j], up_s.at[0], up_r.at[j], place(t, q)).wait_recv()
-
-    got = pieces.at[t * sub + other]
-    remote(got, got, own_s, own_r, sibling).wait_recv()
-    for r in range(1, tp):
-        peer = peer_of(r)
-        for k in range(1, owners):
-            source = lax.rem(q + k, owners)
-            got = part_of(peer * sub + source // dp, lax.rem(source, dp))
-            remote(
-                got, got, forward_s.at[r, k], forward_r.at[peer, source], place(t, source)
-            ).wait_recv()
-
-    piece_rows = pieces.shape[2]
-    for j in range(rows // piece_rows):
-        wanted = t * (rows // piece_rows) + j
-        found = jnp.int32(0)
-        for k in range(pieces.shape[0]):
-            found = jnp.where(owner_ref[k] == wanted, k, found)
-        down_local[:, j * piece_rows : (j + 1) * piece_rows] = pieces[found]
-
-    base_copy.wait()
-    norm_acc[...] = jnp.zeros_like(norm_acc)
-    block = 256
-    up_all = jnp.concatenate([up[j] for j in range(sub)], axis=1)
-
-    def merge(c, carry):
-        here = pl.ds(pl.multiple_of(c * block, block), block)
-        down_rows = down_local[:, here]
-        for n in range(columns // block):
-            cols = slice(n * block, (n + 1) * block)
-            tile = base[here, cols].astype(f32) + lax.dot_general(
-                down_rows, up_all[:, cols], (((0,), (0,)), ((), ())), preferred_element_type=f32
-            )
-            norm_acc[:, cols] += jnp.sum((tile * tile).reshape(block // 8, 8, block), axis=0)
-            combined[here, cols] = tile.astype(bf16)
-        return carry
-
-    lax.fori_loop(0, rows // block, merge, 0)
-    norm_send[...] = jnp.sum(norm_acc[...], axis=0, keepdims=True)
-
-    def result_copy(src, dst, send, recv, k):
-        return remote(
-            src, dst.at[t], send.at[k], recv.at[t], place(q, lax.rem(q + k, owners))
-        )
-
-    itself = t == q
-
-    def norm_copy(k):
-        return result_copy(norm_send, norm_recv, norm_s, norm_r, k)
-
-    for k in range(1, owners):
-        norm_copy(k).start()
-
-    @pl.when(jnp.logical_not(itself))
-    def _():
-        norm_copy(0).start()
-
-    @pl.when(itself)
-    def _():
-        norm_recv[t] = norm_send[...]
-
     fresh = [
         [
             fresh_ref[
@@ -467,6 +401,72 @@
         )
         copy.start()
         context_copies.append(copy)
+    for j in range(sub):
+
+        @pl.when(jnp.logical_or(t != q, s != j))
+        def _():
+            remote(up_ref, up.at[j], up_s.at[0], up_r.at[j], place(t, q)).wait_recv()
+
+    got = pieces.at[t * sub + other]
+    remote(got, got, own_s, own_r, sibling).wait_recv()
+    for r in range(1, tp):
+        peer = peer_of(r)
+        for k in range(1, owners):
+            source = lax.rem(q + k, owners)
+            got = part_of(peer * sub + source // dp, lax.rem(source, dp))
+            remote(
+                got, got, forward_s.at[r, k], forward_r.at[peer, source], place(t, source)
+            ).wait_recv()
+
+    piece_rows = pieces.shape[2]
+    for j in range(rows // piece_rows):
+        wanted = t * (rows // piece_rows) + j
+        found = jnp.int32(0)
+        for k in range(pieces.shape[0]):
+            found = jnp.where(owner_ref[k] == wanted, k, found)
+        down_local[:, j * piece_rows : (j + 1) * piece_rows] = pieces[found]
+
+    base_copy.wait()
+    norm_acc[...] = jnp.zeros_like(norm_acc)
+    block = 256
+    up_all = jnp.concatenate([up[j] for j in range(sub)], axis=1)
+
+    def merge(c, carry):
+        here = pl.ds(pl.multiple_of(c * block, block), block)
+        down_rows = down_local[:, here]
+        for n in range(columns // block):
+            cols = slice(n * block, (n + 1) * block)
+            tile = base[here, cols].astype(f32) + lax.dot_general(
+                down_rows, up_all[:, cols], (((0,), (0,)), ((), ())), preferred_element_type=f32
+            )
+            norm_acc[:, cols] += jnp.sum((tile * tile).reshape(block // 8, 8, block), axis=0)
+            combined[here, cols] = tile.astype(bf16)
+        return carry
+
+    lax.fori_loop(0, rows // block, merge, 0)
+    norm_send[...] = jnp.sum(norm_acc[...], axis=0, keepdims=True)
+
+    def result_copy(src, dst, send, recv, k):
+        return remote(
+            src, dst.at[t], send.at[k], recv.at[t], place(q, lax.rem(q + k, owners))
+        )
+
+    itself = t == q
+
+    def norm_copy(k):
+        return result_copy(norm_send, norm_recv, norm_s, norm_r, k)
+
+    for k in range(1, owners):
+        norm_copy(k).start()
+
+    @pl.when(jnp.logical_not(itself))
+    def _():
+        norm_copy(0).start()
+
+    @pl.when(itself)
+    def _():
+        norm_recv[t] = norm_send[...]
+
     for k in range(1, owners):
         peer = lax.rem(q + k, owners)
         remote(

time: 31.2 us -> 28.9 us (0.926)
  Pallas kernels: 29.6 us -> 27.3 us
    pallas_call x1, Pallas kernels: 29.6 us -> 27.3 us  [fused_local(): pl.pallas_call(functools.partial(fused_kernel, sizes), out_shape=jax.Shap...]
where the time goes in v3:
time: 28.9 us; the launch traced here: 28.6 us
  Pallas kernels  27.3 us (94%)
  local copies, waits for them, and re-layouts  1.31 us (5%)
    pallas_call x1, Pallas kernels, fused_local(): pl.pallas_call(functools.partial(fused_kernel, sizes), out_shape=jax.Shap...  27.3 us
    unnamed x1, local copies, waits for them, and re-layouts  1.31 us

profile of v3, /device:TPU:0, one launch (start us, length us, event | category | flops | bytes accessed | tf_op | source)
XLA Modules:
  0.0 28.6 jit_solution(15539940520739573345)
XLA Ops:
  0.0 27.3 %shard_map.91 = bf16[4,1280]{1,0:T(4,128)(2,1)} custom-call(s32[4]{0:T(128)} %lengths_ref.1, s32[8]{0:T(128)} %owner_ref.1, bf16[4,2048]{1,0:T(4,128)(2,1)} %query_ref.1, bf16[4,2,1024]{2,1,0:T(2,128)(2,1)} %fresh_ref.1, bf16[16,1024]{1,0:T(8,128)(2,1)} %down_ref.1, bf16[16,640]{1,0:T(8,128)(2,1)} %up_ref.1, bf16[640]{0:T(1024)(128)(2,1)} %magnitude_ref.1, ...), custom_call_target="tpu_custom_call" | custom-call | tf_op jit(solution)/shard_map/pallas_call | solution.py:587
  27.3 1.3 %copy.11 = bf16[4,1280]{1,0:T(4,128)(2,1)} copy(bf16[4,1280]{1,0:T(4,128)(2,1)} %shard_map.91) | data formatting | bytes 20480

commit v4 on v3

--- a/solution.py
+++ b/solution.py
@@ -133,6 +133,7 @@
     norm_acc,
     norm_send,
     norm_recv,
+    proj_f32,
     proj_send,
     proj_recv,
     cache_sem,
@@ -201,6 +202,7 @@
     )
     base_copy.start()
 
+    proj_f32[...] = jnp.zeros_like(proj_f32)
     barrier = pltpu.get_barrier_semaphore()
     greeted = [place(peer_of(r), q) for r in range(1, tp)]
     greeted += [place(t, lax.rem(q + k, owners)) for k in range(1, owners)]
@@ -484,6 +486,28 @@
         axis=1,
     )
     middle = columns // 2
+    def proj_copy(side, k):
+        return remote(
+            proj_send.at[side, lax.rem(q + k, owners)],
+            proj_recv.at[side, t],
+            proj_s.at[side, k],
+            proj_r.at[side, t],
+            place(q, lax.rem(q + k, owners)),
+        )
+
+    def send_side(side):
+        proj_send[side] = proj_f32[side].astype(proj_send.dtype)
+        for k in range(1, owners):
+            proj_copy(side, k).start()
+
+        @pl.when(jnp.logical_not(itself))
+        def _():
+            proj_copy(side, 0).start()
+
+        @pl.when(itself)
+        def _():
+            proj_recv[side, t] = proj_send[side, q]
+
     for n in range(columns // block):
         partial = jnp.dot(
             context, combined[:, n * block : (n + 1) * block], preferred_element_type=f32
@@ -492,25 +516,12 @@
             start = n * block + piece * HD
             side, lane = start // middle, start % middle
             for k in range(owners):
-                proj_send[k, side * seqs : (side + 1) * seqs, lane : lane + HD] = partial[
+                proj_f32[side, k, lane // HD * seqs : (lane // HD + 1) * seqs, :] = partial[
                     k * seqs : (k + 1) * seqs, piece * HD : (piece + 1) * HD
                 ]
-
-    def proj_copy(k):
-        return result_copy(
-            proj_send.at[lax.rem(q + k, owners)], proj_recv, proj_s, proj_r, k
-        )
-
-    for k in range(1, owners):
-        proj_copy(k).start()
-
-    @pl.when(jnp.logical_not(itself))
-    def _():
-        proj_copy(0).start()
-
-    @pl.when(itself)
-    def _():
-        proj_recv[t] = proj_send[q]
+        for side in range(2):
+            if n * block < (side + 1) * middle <= (n + 1) * block:
+                send_side(side)
 
     remote(
         magnitudes.at[other], magnitudes.at[other], mag_s, mag_r, sibling
@@ -528,15 +539,17 @@
     for k in range(1, tp):
         squares = squares + norm_recv[k]
     norms = jnp.sqrt(squares + norm_eps)
-    arrived(proj_send.at[0], proj_recv, proj_s, proj_r)
-    total = proj_recv[0]
-    for k in range(1, tp):
-        total = total + proj_recv[k]
     for side in range(2):
+        arrived(proj_send.at[side, 0], proj_recv.at[side], proj_s.at[side], proj_r.at[side])
+        total = proj_recv[side, 0].astype(f32)
+        for k in range(1, tp):
+            total = total + proj_recv[side, k].astype(f32)
         scale = magnitudes[side] / norms[:, side * middle : (side + 1) * middle]
-        out_ref[:, side * middle : (side + 1) * middle] = (
-            total[side * seqs : (side + 1) * seqs] * scale
-        ).astype(bf16)
+        for n in range(middle // HD):
+            lanes = slice(n * HD, (n + 1) * HD)
+            out_ref[:, side * middle + n * HD : side * middle + (n + 1) * HD] = (
+                total[n * seqs : (n + 1) * seqs] * scale[:, lanes]
+            ).astype(bf16)
 
     for copy in query_copies + piece_copies + forward_copies + part_copies + context_copies:
         copy.wait_send()
@@ -552,12 +565,14 @@
 
     for k in range(1, owners):
         norm_copy(k).wait_send()
-        proj_copy(k).wait_send()
+        for side in range(2):
+            proj_copy(side, k).wait_send()
 
     @pl.when(jnp.logical_not(itself))
     def _():
         norm_copy(0).wait_send()
-        proj_copy(0).wait_send()
+        for side in range(2):
+            proj_copy(side, 0).wait_send()
 
 
 def fused_local(
@@ -579,6 +594,7 @@
     rows, width = frozen_base_matrix.shape
     columns = width // owners
     trainers = tp * sub
+    sent_rows = -(-(columns // 2 // HD * seqs) // 16) * 16
     f32, bf16 = jnp.float32, jnp.bfloat16
     sem = pltpu.SemaphoreType.DMA
     vmem = pl.BlockSpec(memory_space=pltpu.VMEM)
@@ -606,8 +622,9 @@
             pltpu.VMEM((8, columns), f32),
             pltpu.VMEM((1, columns), f32),
             pltpu.VMEM((tp, 1, columns), f32),
-            pltpu.VMEM((owners, 2 * seqs, columns // 2), f32),
-            pltpu.VMEM((tp, 2 * seqs, columns // 2), f32),
+            pltpu.VMEM((2, owners, sent_rows, HD), f32),
+            pltpu.VMEM((2, owners, sent_rows, HD), bf16),
+            pltpu.VMEM((2, tp, sent_rows, HD), bf16),
             sem((2,)),
             sem,
             sem((tp,)),
@@ -628,8 +645,8 @@
             sem((owners,)),
             sem((owners,)),
             sem((tp,)),
-            sem((owners,)),
-            sem((tp,)),
+            sem((2, owners)),
+            sem((2, tp)),
         ],
         compiler_params=pltpu.CompilerParams(
             collective_id=0, has_side_effects=True, vmem_limit_bytes=56 * 1024 * 1024

time: 28.9 us -> 28.2 us (0.976)
  Pallas kernels: 27.3 us -> 26.6 us
    pallas_call x1, Pallas kernels: 27.3 us -> 26.6 us  [fused_local(): pl.pallas_call(functools.partial(fused_kernel, sizes), out_shape=jax.Shap...]
where the time goes in v4:
time: 28.2 us; the launch traced here: 27.9 us
  Pallas kernels  26.6 us (94%)
  local copies, waits for them, and re-layouts  1.31 us (5%)
    pallas_call x1, Pallas kernels, fused_local(): pl.pallas_call(functools.partial(fused_kernel, sizes), out_shape=jax.Shap...  26.6 us
    unnamed x1, local copies, waits for them, and re-layouts  1.31 us

profile of v4, /device:TPU:0, one launch (start us, length us, event | category | flops | bytes accessed | tf_op | source)
XLA Modules:
  0.0 27.9 jit_solution(15836979714316552993)
XLA Ops:
  0.0 26.6 %shard_map.91 = bf16[4,1280]{1,0:T(4,128)(2,1)} custom-call(s32[4]{0:T(128)} %lengths_ref.1, s32[8]{0:T(128)} %owner_ref.1, bf16[4,2048]{1,0:T(4,128)(2,1)} %query_ref.1, bf16[4,2,1024]{2,1,0:T(2,128)(2,1)} %fresh_ref.1, bf16[16,1024]{1,0:T(8,128)(2,1)} %down_ref.1, bf16[16,640]{1,0:T(8,128)(2,1)} %up_ref.1, bf16[640]{0:T(1024)(128)(2,1)} %magnitude_ref.1, ...), custom_call_target="tpu_custom_call" | custom-call | tf_op jit(solution)/shard_map/pallas_call | solution.py:603
  26.6 1.3 %copy.11 = bf16[4,1280]{1,0:T(4,128)(2,1)} copy(bf16[4,1280]{1,0:T(4,128)(2,1)} %shard_map.91) | data formatting | bytes 20480
